TPU v7x, 32 devices: a whole 2x2x4 slice. The times are simulated.
32 devices in a mesh: parts: 2 (over y), lon: 16 (over z, x, core).
Axes of the slice: x: 2, y: 2, z: 4, core: 2. Of those that a mesh axis runs over, the one named last changes fastest.
Arguments:
- grid_latents: bfloat16 [32768, 512], P(('parts', 'lon')), parts along dimension 0, may hold values from -6 to 6
- mesh_latents: bfloat16 [8192, 512], P(('parts', 'lon')), parts along dimension 0, may hold values from -6 to 6
- send_block: int32 [32, 4], P(('parts', 'lon')), parts along dimension 0, may hold values from 0 to 7
- send_live: int32 [32, 4], P(('parts', 'lon')), parts along dimension 0, may hold values from 0 to 1
- grid_edge_source: int32 [131072], P(('parts', 'lon')), parts along dimension 0, may hold values from 0 to 1535, as said below
- grid_edge_geometry: float32 [4, 131072], P(None, ('parts', 'lon')), parts along dimension 1, may hold values from -1 to 1
- mesh_edge_source: int32 [65536], P(('parts', 'lon')), parts along dimension 0, may hold values from 0 to 895
- mesh_edge_geometry: float32 [4, 65536], P(None, ('parts', 'lon')), parts along dimension 1, may hold values from -1 to 1
- encode_sender: bfloat16 [512, 512], replicated, may hold values from -0.25 to 0.25
- encode_receiver: bfloat16 [512, 512], replicated, may hold values from -0.25 to 0.25
- encode_geometry: float32 [4, 512], replicated, may hold values from -3 to 3
- encode_edge: bfloat16 [512, 512], replicated, may hold values from -0.25 to 0.25
- encode_gather: bfloat16 [512, 512], replicated, may hold values from -0.25 to 0.25
- encode_self: bfloat16 [512, 512], replicated, may hold values from -0.25 to 0.25
- encode_output: bfloat16 [512, 512], replicated, may hold values from -0.25 to 0.25
- process_sender: bfloat16 [2, 512, 512], replicated, may hold values from -0.25 to 0.25
- process_receiver: bfloat16 [2, 512, 512], replicated, may hold values from -0.25 to 0.25
- process_geometry: float32 [2, 4, 512], replicated, may hold values from -3 to 3
- process_edge: bfloat16 [2, 512, 512], replicated, may hold values from -0.25 to 0.25
- process_gather: bfloat16 [2, 512, 512], replicated, may hold values from -0.25 to 0.25
- process_self: bfloat16 [2, 512, 512], replicated, may hold values from -0.25 to 0.25
- process_output: bfloat16 [2, 512, 512], replicated, may hold values from -0.25 to 0.25
Outputs:
- mesh_out: bfloat16 [8192, 512], P(('parts', 'lon')), parts along dimension 0
There are 2 independent parts, one for each index of `parts`. A program takes and returns all parts, laid end to end along the dimension named above; an argument that names none is the same for every part. Nothing has to cross between parts.
Inputs may be any that keep to these rules, and one draw needn't show every extreme that they name: `grid_edge_source`: indices at or above 1024 point into slot k = (index - 1024) // 128 and only where send_live of the sending device (d - o_k) mod 16 is 1 in slot k.
All inputs are finite; a program needn't handle non-finite values.
Results may differ from a plain program's by a relative error of at most 0.012.
Values may be sent and summed in bfloat16 or wider, within the bound.
A program may use at most 64 MiB of HBM per device.

v0:
```python
import jax
import jax.numpy as jnp
from jax import lax
from jax.sharding import PartitionSpec as P

BLOCK = 128
COARSE_DEV = 8


def shifted(array, axis, by):
    peers = lax.axis_size(axis)
    return lax.ppermute(array, axis, [(i, (i + by) % peers) for i in range(peers)])


def extended(cells, sides, width):
    for axis, dim in sides:
        count = lax.axis_size(axis)
        head = lax.slice_in_dim(cells, 0, width, axis=dim)
        tail = lax.slice_in_dim(cells, cells.shape[dim] - width, cells.shape[dim], axis=dim)
        cells = jnp.concatenate(
            [
                lax.ppermute(tail, axis, [(i, (i + 1) % count) for i in range(count)]),
                cells,
                lax.ppermute(head, axis, [((i + 1) % count, i) for i in range(count)]),
            ],
            axis=dim,
        )
    return cells


def layer_norm(values):
    center = jnp.mean(values, axis=-1, keepdims=True)
    centred = values - center
    spread = jnp.mean(centred * centred, axis=-1, keepdims=True)
    return centred * lax.rsqrt(spread + 1e-05)


def interact(
    visible, receivers, source, geometry, w_receive, w_geometry, w_edge, w_gather, w_self, w_output
):
    node_count, width = receivers.shape
    degree = source.shape[0] // node_count
    pulled = jnp.dot(receivers, w_receive, preferred_element_type=jnp.float32)
    spread_pull = jnp.broadcast_to(pulled[:, None, :], (node_count, degree, width)).reshape(
        -1, width
    )
    shape_term = jnp.einsum("ke,kd->ed", geometry, w_geometry, precision=lax.Precision.HIGHEST)
    joined = jax.nn.silu(visible[source].astype(jnp.float32) + spread_pull + shape_term).astype(
        jnp.bfloat16
    )
    message = layer_norm(jnp.dot(joined, w_edge, preferred_element_type=jnp.float32)).astype(
        jnp.bfloat16
    )
    summed = jnp.sum(message.astype(jnp.float32).reshape(node_count, degree, width), axis=1).astype(
        jnp.bfloat16
    )
    update = jax.nn.silu(
        jnp.dot(summed, w_gather, preferred_element_type=jnp.float32)
        + jnp.dot(receivers, w_self, preferred_element_type=jnp.float32)
    ).astype(jnp.bfloat16)
    output = layer_norm(jnp.dot(update, w_output, preferred_element_type=jnp.float32))
    return (receivers.astype(jnp.float32) + output).astype(jnp.bfloat16)


def local(
    grid_latents,
    mesh_latents,
    send_block,
    send_live,
    grid_edge_source,
    grid_edge_geometry,
    mesh_edge_source,
    mesh_edge_geometry,
    encode_sender,
    encode_receiver,
    encode_geometry,
    encode_edge,
    encode_gather,
    encode_self,
    encode_output,
    process_sender,
    process_receiver,
    process_geometry,
    process_edge,
    process_gather,
    process_self,
    process_output,
):
    width = grid_latents.shape[1]
    slot_count = send_block.shape[1]
    offsets = [(slot // 2 + 1) * (1 - 2 * (slot % 2)) for slot in range(slot_count)]
    live_scale = send_live[0][:, None, None].astype(jnp.bfloat16)
    projected = jnp.dot(grid_latents, encode_sender, preferred_element_type=jnp.float32).astype(
        jnp.bfloat16
    )
    blocks = projected.reshape(-1, BLOCK, width)
    outgoing = blocks[send_block[0]] * live_scale
    arrived = jnp.stack(
        [shifted(outgoing[slot], "lon", offsets[slot]) for slot in range(slot_count)]
    )
    arrived = arrived.reshape(-1, width)
    visible = jnp.concatenate([projected, arrived], axis=0)
    latents = interact(
        visible,
        mesh_latents,
        grid_edge_source,
        grid_edge_geometry,
        encode_receiver,
        encode_geometry,
        encode_edge,
        encode_gather,
        encode_self,
        encode_output,
    )
    for step in range(process_sender.shape[0]):
        mesh_projected = jnp.dot(
            latents, process_sender[step], preferred_element_type=jnp.float32
        ).astype(jnp.bfloat16)
        nearby = extended(mesh_projected, (("lon", 0),), mesh_projected.shape[0])
        coarse = lax.all_gather(mesh_projected[:COARSE_DEV], "lon", axis=0, tiled=True)
        visible = jnp.concatenate([nearby, coarse], axis=0)
        latents = interact(
            visible,
            latents,
            mesh_edge_source,
            mesh_edge_geometry,
            process_receiver[step],
            process_geometry[step],
            process_edge[step],
            process_gather[step],
            process_self[step],
            process_output[step],
        )
    return latents


def solution(mesh):
    placed = (
        P(("parts", "lon"), None),
        P(("parts", "lon"), None),
        P(("parts", "lon"), None),
        P(("parts", "lon"), None),
        P(("parts", "lon")),
        P(None, ("parts", "lon")),
        P(("parts", "lon")),
        P(None, ("parts", "lon")),
        P(),
        P(),
        P(),
        P(),
        P(),
        P(),
        P(),
        P(),
        P(),
        P(),
        P(),
        P(),
        P(),
        P(),
    )
    return jax.shard_map(
        local, mesh=mesh, in_specs=placed, out_specs=P(("parts", "lon"), None), check_vma=False
    )
```

profile of v0, /device:TPU:0, one launch (start us, length us, event | category | flops | bytes accessed | tf_op | source)
XLA Modules:
  0.0 155.2 jit_solution(16701703914154395832)
XLA Ops:
  1.4 1.7 %convolution_convert_fusion = bf16[1024,512]{1,0:T(8,128)(2,1)S(1)} fusion(bf16[1024,512]{1,0:T(8,128)(2,1)S(1)} %copy-done, bf16[512,512]{1,0:T(8,128)(2,1)} %param.30), kind=kOutput, calls=%fused_computation.27 | convolution fusion | flops 537395200 | bytes 2621440 | tf_op jit(solution)/shard_map/dot_general | solution.py:93
  3.9 6.0 %collective-permute-start.3 = (bf16[128,512]{1,0:T(8,128)(2,1)S(1)}, bf16[128,512]{1,0:T(8,128)(2,1)S(1)}, u32[]{:S(2)}, u32[]{:S(2)}) collective-permute-start(bf16[128,512]{1,0:T(8,128)(2,1)S(1)} %get-tuple-element.6), channel_id=1, source_target_pairs={{0,14},{1,15},{2,0},{3,1},{4,2},{5,3},{6,4},{7,5},{8,6},{9,7},{10,... | collective-permute-start | bytes 393224 | tf_op jit(solution)/shard_map/ppermute | solution.py:12
  10.0 4.4 %collective-permute-start.1 = (bf16[128,512]{1,0:T(8,128)(2,1)S(1)}, bf16[128,512]{1,0:T(8,128)(2,1)S(1)}, u32[]{:S(2)}, u32[]{:S(2)}) collective-permute-start(bf16[128,512]{1,0:T(8,128)(2,1)S(1)} %get-tuple-element.8), channel_id=1, source_target_pairs={{0,15},{1,0},{2,1},{3,2},{4,3},{5,4},{6,5},{7,6},{8,7},{9,8},{10,9... | collective-permute-start | bytes 393224 | tf_op jit(solution)/shard_map/ppermute | solution.py:12
  14.5 5.1 %fusion.57 = f32[2048,512]{1,0:T(8,128)} fusion(f32[4,2048]{1,0:T(4,128)S(1)} %copy-done.11, f32[2,4,512]{2,1,0:T(4,128)S(1)} %copy-done.13), kind=kOutput, calls=%fused_computation.91 | convolution fusion | flops 50331648 | bytes 4235264 | tf_op jit(solution)/shard_map/ke,kd->ed/dot_general | solution.py:47
  19.6 5.0 %fusion.55 = f32[2048,512]{1,0:T(8,128)} fusion(f32[4,2048]{1,0:T(4,128)S(1)} %copy-done.11, f32[2,4,512]{2,1,0:T(4,128)S(1)} %copy-done.13), kind=kOutput, calls=%fused_computation.89 | convolution fusion | flops 50331648 | bytes 4235264 | tf_op jit(solution)/shard_map/ke,kd->ed/dot_general | solution.py:47
  25.1 1.3 pad_maximum_fusion
  26.5 17.3 %gather_fusion.1 = bf16[4096,512]{1,0:T(8,128)(2,1)} fusion(bf16[1536,512]{1,0:T(8,128)(2,1)S(1)} %pad_maximum_fusion, s32[4096]{0:T(1024)S(1)} %fusion.53), kind=kCustom, calls=%fused_computation.1 | custom fusion | bytes 8404992 | tf_op jit(solution)/shard_map/gather | solution.py:48
  43.8 10.7 %multiply_convert_fusion.1 = bf16[4096,512]{1,0:T(8,128)(2,1)S(1)} fusion(bf16[4096,512]{1,0:T(8,128)(2,1)} %gather_fusion.1, f32[4,4096]{1,0:T(4,128)S(1)} %copy-done.12, f32[4,512]{1,0:T(4,128)S(1)} %copy-done.15, f32[256,512]{1,0:T(8,128)S(1)} %fusion.77), kind=kOutput, calls=%fused_computation.8 | convolution fusion | flops 117440512 | bytes 8986624 | tf_op jit(solution)/shard_map/ke,kd->ed/dot_general | solution.py:47
  54.5 2.4 %fusion.67 = (f32[4096]{0:T(1024)S(1)}, f32[4096,512]{1,0:T(8,128)S(1)}) fusion(bf16[4096,512]{1,0:T(8,128)(2,1)S(1)} %multiply_convert_fusion.1, bf16[512,512]{1,0:T(8,128)(2,1)S(1)} %copy-done.7), kind=kOutput, calls=%fused_computation.115 | convolution fusion | flops 2149576704 | bytes 13123584 | tf_op jit(solution)/shard_map/dot_general | solution.py:51
  56.9 1.4 multiply_reduce_fusion
  58.4 2.1 %bitcast_reduce_fusion = bf16[256,512]{1,0:T(8,128)(2,1)S(1)} fusion(f32[4096]{0:T(1024)S(1)} %add_rsqrt_fusion, f32[4096,512]{1,0:T(8,128)S(1)} %get-tuple-element.10, f32[4096]{0:T(1024)S(1)} %broadcast_multiply_fusion.1), kind=kLoop, calls=%fused_computation.13 | loop fusion | flops 8257536 | bytes 8683520 | tf_op jit(solution)/shard_map/reduce_sum | solution.py:54
  60.5 1.1 fusion.78
  61.7 2.0 %fusion.68 = (f32[256]{0:T(256)S(1)}, f32[256,512]{1,0:T(8,128)S(1)}) fusion(bf16[512,512]{1,0:T(8,128)(2,1)} %param.36, f32[256,512]{1,0:T(8,128)} %fusion.78, bf16[256,512]{1,0:T(8,128)(2,1)S(1)} %copy-done.6, bf16[512,512]{1,0:T(8,128)(2,1)} %param.35), kind=kOutput, calls=%fused_computation.116 | convolution fusion | flops 269352704 | bytes 2360320 | tf_op jit(solution)/shard_map/dot_general | solution.py:61
  64.1 1.3 convolution_convert_fusion.2
  65.5 4.4 %collective-permute-start.5 = (bf16[256,512]{1,0:T(8,128)(2,1)S(1)}, bf16[256,512]{1,0:T(8,128)(2,1)S(1)}, u32[]{:S(2)}, u32[]{:S(2)}) collective-permute-start(bf16[256,512]{1,0:T(8,128)(2,1)S(1)} %convolution_convert_fusion.2), channel_id=1, source_target_pairs={{1,0},{2,1},{3,2},{4,3},{5,4},{6,5},{7,6},{8,7},{9,8},{10,9},{11,1... | collective-permute-start | bytes 786440 | tf_op jit(solution)/shard_map/ppermute | solution.py:24
  69.9 19.8 %all_gather.6 = bf16[128,512]{1,0:T(8,128)(2,1)S(1)} all-gather(bf16[8,512]{1,0:T(8,128)(2,1)S(1)} %slice.92), channel_id=1, replica_groups=mesh['parts'=2,'lon'=16] {'lon'}, dimensions={0}, use_global_device_ids=true | all-gather | bytes 139264 | tf_op jit(solution)/shard_map/all_gather | solution.py:120
  89.7 1.1 fusion.24
  90.9 9.2 %gather_fusion.2 = bf16[2048,512]{1,0:T(8,128)(2,1)} fusion(bf16[896,512]{1,0:T(8,128)(2,1)S(1)} %pad_maximum_fusion.1, s32[2048]{0:T(1024)S(1)} %fusion.54), kind=kCustom, calls=%fused_computation.2 | custom fusion | bytes 4202496 | tf_op jit(solution)/shard_map/gather | solution.py:48
  100.1 4.2 %fusion.69 = (f32[2048]{0:T(1024)S(1)}, f32[2048,512]{1,0:T(8,128)S(1)}) fusion(bf16[2,512,512]{2,1,0:T(8,128)(2,1)} %param.40, f32[2048,512]{1,0:T(8,128)} %fusion.57, bf16[2048,512]{1,0:T(8,128)(2,1)} %gather_fusion.2, f32[256,512]{1,0:T(8,128)} %fusion.24), kind=kOutput, calls=%fused_computation.117 | convolution fusion | flops 1083176960 | bytes 11542528 | tf_op jit(solution)/shard_map/dot_general | solution.py:51
  104.3 0.8 multiply_reduce_fusion.2
  105.2 1.7 %fusion.4 = bf16[256,512]{1,0:T(8,128)(2,1)S(1)} fusion(f32[2048,512]{1,0:T(8,128)S(1)} %get-tuple-element.14, f32[2048]{0:T(1024)S(1)} %add_rsqrt_fusion.2, f32[2048]{0:T(1024)S(1)} %broadcast_multiply_fusion.3), kind=kLoop, calls=%fused_computation.21 | loop fusion | flops 4063232 | bytes 4472832 | tf_op jit(solution)/shard_map/reduce_sum | solution.py:54
  107.3 1.9 %fusion.70 = (f32[256]{0:T(256)S(1)}, f32[256,512]{1,0:T(8,128)S(1)}) fusion(bf16[2,512,512]{2,1,0:T(8,128)(2,1)} %param.43, f32[256,512]{1,0:T(8,128)S(1)} %fusion.21, bf16[256,512]{1,0:T(8,128)(2,1)S(1)} %add_convert_fusion.2, bf16[2,512,512]{2,1,0:T(8,128)(2,1)} %param.42), kind=kOutput, calls=%fused_computation.118 | convolution fusion | flops 269352704 | bytes 2360320 | tf_op jit(solution)/shard_map/dot_general | solution.py:61
  109.5 1.3 convolution_convert_fusion.1
  111.3 4.1 %collective-permute-start.7 = (bf16[256,512]{1,0:T(8,128)(2,1)S(1)}, bf16[256,512]{1,0:T(8,128)(2,1)S(1)}, u32[]{:S(2)}, u32[]{:S(2)}) collective-permute-start(bf16[256,512]{1,0:T(8,128)(2,1)S(1)} %convolution_convert_fusion.1), channel_id=1, source_target_pairs={{1,0},{2,1},{3,2},{4,3},{5,4},{6,5},{7,6},{8,7},{9,8},{10,9},{11,1... | collective-permute-start | bytes 786440 | tf_op jit(solution)/shard_map/ppermute | solution.py:24
  115.4 19.7 %all_gather.7 = bf16[128,512]{1,0:T(8,128)(2,1)S(1)} all-gather(bf16[8,512]{1,0:T(8,128)(2,1)S(1)} %slice.93), channel_id=1, replica_groups=mesh['parts'=2,'lon'=16] {'lon'}, dimensions={0}, use_global_device_ids=true | all-gather | bytes 139264 | tf_op jit(solution)/shard_map/all_gather | solution.py:120
  135.0 1.1 fusion.15
  136.2 9.2 %gather_fusion.3 = bf16[2048,512]{1,0:T(8,128)(2,1)} fusion(bf16[896,512]{1,0:T(8,128)(2,1)S(1)} %pad_maximum_fusion.2, s32[2048]{0:T(1024)S(1)} %fusion.54), kind=kCustom, calls=%fused_computation.3 | custom fusion | bytes 4202496 | tf_op jit(solution)/shard_map/gather | solution.py:48
  145.4 3.8 %fusion.73 = (f32[2048]{0:T(1024)S(1)}, f32[2048,512]{1,0:T(8,128)S(1)}) fusion(bf16[2,512,512]{2,1,0:T(8,128)(2,1)} %param.40, f32[2048,512]{1,0:T(8,128)} %fusion.55, bf16[2048,512]{1,0:T(8,128)(2,1)} %gather_fusion.3, f32[256,512]{1,0:T(8,128)S(1)} %copy-done.10), kind=kOutput, calls=%fused_computation.119 | convolution fusion | flops 1083176960 | bytes 11542528 | tf_op jit(solution)/shard_map/dot_general | solution.py:51
  149.3 0.8 multiply_reduce_fusion.1
  150.2 1.7 %fusion.6 = bf16[256,512]{1,0:T(8,128)(2,1)S(1)} fusion(f32[2048,512]{1,0:T(8,128)S(1)} %get-tuple-element.18, f32[2048]{0:T(1024)S(1)} %add_rsqrt_fusion.1, f32[2048]{0:T(1024)S(1)} %broadcast_multiply_fusion.2), kind=kLoop, calls=%fused_computation.23 | loop fusion | flops 4063232 | bytes 4472832 | tf_op jit(solution)/shard_map/reduce_sum | solution.py:54
  152.2 1.9 %fusion.74 = (f32[256]{0:T(256)S(1)}, f32[256,512]{1,0:T(8,128)S(1)}) fusion(bf16[2,512,512]{2,1,0:T(8,128)(2,1)} %param.43, f32[256,512]{1,0:T(8,128)S(1)} %fusion.12, bf16[256,512]{1,0:T(8,128)(2,1)S(1)} %add_convert_fusion.1, bf16[2,512,512]{2,1,0:T(8,128)(2,1)} %param.42), kind=kOutput, calls=%fused_computation.120 | convolution fusion | flops 269352704 | bytes 2360320 | tf_op jit(solution)/shard_map/dot_general | solution.py:61
  154.3 0.9 add_convert_fusion
  (79 shorter events, 4.8 us)
Async XLA Ops:
  0.0 1.4 copy-start
  0.0 14.5 %copy-start.11 = (f32[4,2048]{1,0:T(4,128)S(1)}, f32[4,2048]{1,0:T(4,128)}, u32[]{:S(2)}) copy-start(f32[4,2048]{1,0:T(4,128)} %param.29) | copy-start | bytes 98308
  0.0 14.5 %copy-start.13 = (f32[2,4,512]{2,1,0:T(4,128)S(1)}, f32[2,4,512]{2,1,0:T(4,128)}, u32[]{:S(2)}) copy-start(f32[2,4,512]{2,1,0:T(4,128)} %param.39) | copy-start | bytes 49156
  3.2 21.5 %copy-start.1 = (bf16[1024,512]{1,0:T(8,128)(2,1)}, bf16[1024,512]{1,0:T(8,128)(2,1)S(1)}, u32[]{:S(2)}) copy-start(bf16[1024,512]{1,0:T(8,128)(2,1)S(1)} %convolution_convert_fusion) | copy-start | bytes 3145732
  3.9 21.1 %collective-permute-start.3 = (bf16[128,512]{1,0:T(8,128)(2,1)S(1)}, bf16[128,512]{1,0:T(8,128)(2,1)S(1)}, u32[]{:S(2)}, u32[]{:S(2)}) collective-permute-start(bf16[128,512]{1,0:T(8,128)(2,1)S(1)} %get-tuple-element.6), channel_id=1, source_target_pairs={{0,14},{1,15},{2,0},{3,1},{4,2},{5,3},{6,4},{7,5},{8,6},{9,7},{10,... | collective-permute-start | bytes 393224 | tf_op jit(solution)/shard_map/ppermute | solution.py:12
  10.0 15.0 %collective-permute-start = (bf16[128,512]{1,0:T(8,128)(2,1)S(1)}, bf16[128,512]{1,0:T(8,128)(2,1)S(1)}, u32[]{:S(2)}, u32[]{:S(2)}) collective-permute-start(bf16[128,512]{1,0:T(8,128)(2,1)S(1)} %get-tuple-element.5), channel_id=1, source_target_pairs={{0,1},{1,2},{2,3},{3,4},{4,5},{5,6},{6,7},{7,8},{8,9},{9,10},{10,1... | collective-permute-start | bytes 393224 | tf_op jit(solution)/shard_map/ppermute | solution.py:12
  10.0 15.0 %collective-permute-start.1 = (bf16[128,512]{1,0:T(8,128)(2,1)S(1)}, bf16[128,512]{1,0:T(8,128)(2,1)S(1)}, u32[]{:S(2)}, u32[]{:S(2)}) collective-permute-start(bf16[128,512]{1,0:T(8,128)(2,1)S(1)} %get-tuple-element.8), channel_id=1, source_target_pairs={{0,15},{1,0},{2,1},{3,2},{4,3},{5,4},{6,5},{7,6},{8,7},{9,8},{10,9... | collective-permute-start | bytes 393224 | tf_op jit(solution)/shard_map/ppermute | solution.py:12
  14.4 10.2 %copy-start.14 = (s32[4096]{0:T(1024)S(1)}, s32[4096]{0:T(1024)}, u32[]{:S(2)}) copy-start(s32[4096]{0:T(1024)} %param.26) | copy-start | bytes 49156
  14.4 10.2 %copy-start.5 = (bf16[256,512]{1,0:T(8,128)(2,1)S(1)}, bf16[256,512]{1,0:T(8,128)(2,1)}, u32[]{:S(2)}) copy-start(bf16[256,512]{1,0:T(8,128)(2,1)} %param.23) | copy-start | bytes 786436
  14.4 10.2 %copy-start.8 = (bf16[512,512]{1,0:T(8,128)(2,1)S(1)}, bf16[512,512]{1,0:T(8,128)(2,1)}, u32[]{:S(2)}) copy-start(bf16[512,512]{1,0:T(8,128)(2,1)} %param.31) | copy-start | bytes 1572868
  14.4 10.5 %copy-start.16 = (s32[2048]{0:T(1024)S(1)}, s32[2048]{0:T(1024)}, u32[]{:S(2)}) copy-start(s32[2048]{0:T(1024)} %param.28) | copy-start | bytes 24580
  14.4 10.6 %collective-permute-start.2 = (bf16[128,512]{1,0:T(8,128)(2,1)S(1)}, bf16[128,512]{1,0:T(8,128)(2,1)S(1)}, u32[]{:S(2)}, u32[]{:S(2)}) collective-permute-start(bf16[128,512]{1,0:T(8,128)(2,1)S(1)} %get-tuple-element.7), channel_id=1, source_target_pairs={{0,2},{1,3},{2,4},{3,5},{4,6},{5,7},{6,8},{7,9},{8,10},{9,11},{10,... | collective-permute-start | bytes 393224 | tf_op jit(solution)/shard_map/ppermute | solution.py:12
  26.4 17.3 %copy-start.12 = (f32[4,4096]{1,0:T(4,128)S(1)}, f32[4,4096]{1,0:T(4,128)}, u32[]{:S(2)}) copy-start(f32[4,4096]{1,0:T(4,128)} %param.27) | copy-start | bytes 196612
  26.4 17.3 %copy-start.15 = (f32[4,512]{1,0:T(4,128)S(1)}, f32[4,512]{1,0:T(4,128)}, u32[]{:S(2)}) copy-start(f32[4,512]{1,0:T(4,128)} %param.32) | copy-start | bytes 24580
  43.8 10.7 %copy-start.7 = (bf16[512,512]{1,0:T(8,128)(2,1)S(1)}, bf16[512,512]{1,0:T(8,128)(2,1)}, u32[]{:S(2)}) copy-start(bf16[512,512]{1,0:T(8,128)(2,1)} %param.33) | copy-start | bytes 1572868
  58.4 2.1 %copy-start.9 = (bf16[512,512]{1,0:T(8,128)(2,1)S(1)}, bf16[512,512]{1,0:T(8,128)(2,1)}, u32[]{:S(2)}) copy-start(bf16[512,512]{1,0:T(8,128)(2,1)} %param.34) | copy-start | bytes 1572868
  58.4 3.3 %copy-start.6 = (bf16[256,512]{1,0:T(8,128)(2,1)S(1)}, bf16[256,512]{1,0:T(8,128)(2,1)}, u32[]{:S(2)}) copy-start(bf16[256,512]{1,0:T(8,128)(2,1)} %param.23) | copy-start | bytes 786436
  60.5 29.2 %copy-start.2 = (bf16[2,512,512]{2,1,0:T(8,128)(2,1)S(1)}, bf16[2,512,512]{2,1,0:T(8,128)(2,1)}, u32[]{:S(2)}) copy-start(bf16[2,512,512]{2,1,0:T(8,128)(2,1)} %param.38) | copy-start | bytes 3145732
  65.4 25.4 %collective-permute-start.4 = (bf16[256,512]{1,0:T(8,128)(2,1)S(1)}, bf16[256,512]{1,0:T(8,128)(2,1)S(1)}, u32[]{:S(2)}, u32[]{:S(2)}) collective-permute-start(bf16[256,512]{1,0:T(8,128)(2,1)S(1)} %convolution_convert_fusion.2), channel_id=1, source_target_pairs={{0,1},{1,2},{2,3},{3,4},{4,5},{5,6},{6,7},{7,8},{8,9},{9,10},{10,1... | collective-permute-start | bytes 786440 | tf_op jit(solution)/shard_map/ppermute | solution.py:22
  65.5 25.3 %collective-permute-start.5 = (bf16[256,512]{1,0:T(8,128)(2,1)S(1)}, bf16[256,512]{1,0:T(8,128)(2,1)S(1)}, u32[]{:S(2)}, u32[]{:S(2)}) collective-permute-start(bf16[256,512]{1,0:T(8,128)(2,1)S(1)} %convolution_convert_fusion.2), channel_id=1, source_target_pairs={{1,0},{2,1},{3,2},{4,3},{5,4},{6,5},{7,6},{8,7},{9,8},{10,9},{11,1... | collective-permute-start | bytes 786440 | tf_op jit(solution)/shard_map/ppermute | solution.py:24
  104.3 2.6 %copy-start.3 = (bf16[2,512,512]{2,1,0:T(8,128)(2,1)S(1)}, bf16[2,512,512]{2,1,0:T(8,128)(2,1)}, u32[]{:S(2)}) copy-start(bf16[2,512,512]{2,1,0:T(8,128)(2,1)} %param.41) | copy-start | bytes 3145732
  110.9 25.3 %collective-permute-start.6 = (bf16[256,512]{1,0:T(8,128)(2,1)S(1)}, bf16[256,512]{1,0:T(8,128)(2,1)S(1)}, u32[]{:S(2)}, u32[]{:S(2)}) collective-permute-start(bf16[256,512]{1,0:T(8,128)(2,1)S(1)} %convolution_convert_fusion.1), channel_id=1, source_target_pairs={{0,1},{1,2},{2,3},{3,4},{4,5},{5,6},{6,7},{7,8},{8,9},{9,10},{10,1... | collective-permute-start | bytes 786440 | tf_op jit(solution)/shard_map/ppermute | solution.py:22
  111.3 24.9 %collective-permute-start.7 = (bf16[256,512]{1,0:T(8,128)(2,1)S(1)}, bf16[256,512]{1,0:T(8,128)(2,1)S(1)}, u32[]{:S(2)}, u32[]{:S(2)}) collective-permute-start(bf16[256,512]{1,0:T(8,128)(2,1)S(1)} %convolution_convert_fusion.1), channel_id=1, source_target_pairs={{1,0},{2,1},{3,2},{4,3},{5,4},{6,5},{7,6},{8,7},{9,8},{10,9},{11,1... | collective-permute-start | bytes 786440 | tf_op jit(solution)/shard_map/ppermute | solution.py:24
  136.2 9.2 %copy-start.10 = (f32[256,512]{1,0:T(8,128)S(1)}, f32[256,512]{1,0:T(8,128)}, u32[]{:S(2)}) copy-start(f32[256,512]{1,0:T(8,128)} %fusion.15) | copy-start | bytes 1572868
  149.3 2.6 %copy-start.4 = (bf16[2,512,512]{2,1,0:T(8,128)(2,1)S(1)}, bf16[2,512,512]{2,1,0:T(8,128)(2,1)}, u32[]{:S(2)}) copy-start(bf16[2,512,512]{2,1,0:T(8,128)(2,1)} %param.41) | copy-start | bytes 3145732
where the time goes:
time: 156 us; the launch traced here: 155 us
  matrix products  45.8 us (29%)
  blocking collectives  39.4 us (25%)
  local copies, waits for them, and re-layouts  36.3 us (23%)
  starting transfers between devices  19.5 us (12%)
  other arithmetic  13.6 us (9%)
    all_gather x2, blocking collectives, local(): lax.all_gather(mesh_projected[:COARSE_DEV], 'lon', axis=0, tiled=True)  39.4 us
    gather x3, local copies, waits for them, and re-layouts, interact(): visible[source].astype(jnp.float32) + spread_pull + shape_term  35.6 us
    dot_general x3, matrix products, interact(): jnp.einsum('ke,kd->ed', geometry, w_geometry, precision=lax.Precision.HIG...  20.9 us
    ppermute x4, starting transfers between devices, shifted(): lax.ppermute(array, axis, [(i, (i + by) % peers) for i in range(peers)])  10.5 us
    dot_general x3, matrix products, interact(): jnp.dot(joined, w_edge, preferred_element_type=jnp.float32)  10.5 us
    ppermute x2, starting transfers between devices, extended(): lax.ppermute(head, axis, [((i + 1) % count, i) for i in range(count)])  8.54 us
    dot_general x3, matrix products, interact(): jnp.dot(update, w_output, preferred_element_type=jnp.float32)  5.74 us
    reduce_sum x3, other arithmetic, interact(): jnp.sum(message.astype(jnp.float32).reshape(node_count, degree, width), a...  5.58 us
  transfers between devices with their start and end apart: 8, of which 0 were waited for; matrix products, arithmetic and copies ran while one was open for 8% of the time, Pallas kernels for 0%

commit v1 on v0

v1 whole, which is shorter than its diff:
```python
import functools

import jax
import jax.numpy as jnp
from jax import lax
from jax.experimental import pallas as pl
from jax.experimental.pallas import tpu as pltpu
from jax.sharding import PartitionSpec as P

BLOCK = 128
COARSE_DEV = 8
COARSE_ROWS = 16
CHUNK = 64
F32 = jnp.float32
BF16 = jnp.bfloat16


def dot(a, b):
    return jnp.dot(a, b, preferred_element_type=F32)


def silu(v):
    half = 0.5 * v
    return half + half * jnp.tanh(half)


def layer_norm(v):
    centred = v - jnp.mean(v, axis=-1, keepdims=True)
    spread = jnp.mean(centred * centred, axis=-1, keepdims=True)
    return centred * lax.rsqrt(spread + 1e-05)


def node_chunk(
    rows, n, degree, visible, meta_ref, at_index, at_geometry, hot, pulled, own_term, receivers,
    w_geometry, w_edge, w_gather, w_output,
):
    width = pulled.shape[1]
    depth = visible.shape[0]
    meta = meta_ref[rows, :]
    lane = lax.broadcasted_iota(jnp.int32, (n, 128), 1).astype(F32)
    for j in range(degree):
        away = jnp.broadcast_to(meta[:, at_index + j : at_index + j + 1], (n, 128)) - lane
        for tile in range(depth // 128):
            hot[j * n : (j + 1) * n, tile * 128 : (tile + 1) * 128] = jnp.where(
                away == float(tile * 128), 1.0, 0.0
            ).astype(BF16)
    picked = dot(hot[: degree * n, :depth], visible[...])
    base = pulled[rows, :]
    w_g = w_geometry[...]
    joined = []
    for j in range(degree):
        term = picked[j * n : (j + 1) * n] + base
        for k in range(4):
            col = at_geometry + k * degree + j
            term = term + meta[:, col : col + 1] * w_g[k : k + 1, :]
        joined.append(silu(term).astype(BF16))
    message = layer_norm(dot(jnp.concatenate(joined, axis=0), w_edge[...]))
    message = message.astype(BF16).astype(F32)
    summed = message[:n]
    for j in range(1, degree):
        summed = summed + message[j * n : (j + 1) * n]
    update = silu(dot(summed.astype(BF16), w_gather[...]) + own_term[rows, :]).astype(BF16)
    out = layer_norm(dot(update, w_output[...]))
    return (receivers[rows, :].astype(F32) + out).astype(BF16)


def kernel(
    peers, steps, degrees,
    chosen, meta_in, grid_in, mesh_in, *rest,
):
    weights_in = rest[:14]
    out_ref = rest[14]
    (meta, grid, mesh_lat, *weights) = rest[15 : 15 + 17]
    (
        visible, outgoing, mesh_visible, latents, pulled, own_term, hot,
        load_sem, slot_send, slot_recv, near_send, near_recv, far_send, far_recv,
    ) = rest[32:]
    (
        e_sender, e_receiver, e_geometry, e_edge, e_gather, e_self, e_output,
        p_sender, p_receiver, p_geometry, p_edge, p_gather, p_self, p_output,
    ) = weights
    me = lax.axis_index("lon")
    slots = outgoing.shape[0] // BLOCK
    offsets = [(s // 2 + 1) * (1 - 2 * (s % 2)) for s in range(slots)]
    nodes = mesh_lat.shape[0]
    grid_rows = grid.shape[0]
    chunks = nodes // CHUNK

    def peer(by):
        return lax.rem(me + by + peers, peers)

    barrier = pltpu.get_barrier_semaphore()

    def greet(by, carry):
        pl.semaphore_signal(
            barrier, inc=1, device_id={"lon": peer(by)}, device_id_type=pl.DeviceIdType.MESH
        )
        return carry

    lax.fori_loop(1, peers, greet, 0)

    loads = {}
    pairs = {"grid": (grid_in, grid), "meta": (meta_in, meta), "mesh": (mesh_in, mesh_lat)}
    for at in range(14):
        pairs[at] = (weights_in[at], weights[at])
    order = ["grid", 0, "mesh", 1, 5, "meta", 2, 3, 4, 6, 7, 8, 12, 9, 10, 11, 13]
    for at, name in enumerate(order):
        loads[name] = pltpu.make_async_copy(*pairs[name], load_sem.at[at])
        loads[name].start()

    loads["grid"].wait()
    loads[0].wait()
    w_sender = e_sender[...]
    for s in range(slots):
        total = None
        for b in range(grid_rows // BLOCK):
            part = grid[b * BLOCK : (b + 1) * BLOCK, :].astype(F32) * chosen[0, s, b]
            total = part if total is None else total + part
        outgoing[s * BLOCK : (s + 1) * BLOCK, :] = dot(total.astype(BF16), w_sender).astype(BF16)
    pl.semaphore_wait(barrier, peers - 1)
    slot_copies = []
    for s in range(slots):
        copy = pltpu.make_async_remote_copy(
            src_ref=outgoing.at[pl.ds(s * BLOCK, BLOCK)],
            dst_ref=visible.at[pl.ds(grid_rows + s * BLOCK, BLOCK)],
            send_sem=slot_send.at[s],
            recv_sem=slot_recv.at[s],
            device_id={"lon": peer(offsets[s])},
            device_id_type=pl.DeviceIdType.MESH,
        )
        copy.start()
        slot_copies.append(copy)
    visible[:grid_rows, :] = dot(grid[...], w_sender).astype(BF16)
    loads["mesh"].wait()
    loads[1].wait()
    pulled[...] = dot(mesh_lat[...], e_receiver[...])
    loads[5].wait()
    own_term[...] = dot(mesh_lat[...], e_self[...])
    for name in ("meta", 2, 3, 4, 6, 7):
        loads[name].wait()
    for copy in slot_copies:
        copy.wait()

    def near_copy(step, chunk, side):
        landing = 0 if side == 0 else 2 * nodes
        start = pl.multiple_of(chunk * CHUNK, CHUNK)
        return pltpu.make_async_remote_copy(
            src_ref=mesh_visible.at[step, pl.ds(nodes + start, CHUNK)],
            dst_ref=mesh_visible.at[step, pl.ds(landing + start, CHUNK)],
            send_sem=near_send.at[step, side, chunk],
            recv_sem=near_recv.at[step, side, chunk],
            device_id={"lon": peer(1 if side == 0 else -1)},
            device_id_type=pl.DeviceIdType.MESH,
        )

    def far_copy(step, by, sender):
        start = pl.multiple_of(3 * nodes + sender * COARSE_ROWS, COARSE_ROWS)
        return pltpu.make_async_remote_copy(
            src_ref=mesh_visible.at[step, pl.ds(nodes, COARSE_ROWS)],
            dst_ref=mesh_visible.at[step, pl.ds(start, COARSE_ROWS)],
            send_sem=far_send.at[step, by],
            recv_sem=far_recv.at[step, sender],
            device_id={"lon": peer(by)},
            device_id_type=pl.DeviceIdType.MESH,
        )

    def hand_on(step, chunk, fresh):
        start = pl.multiple_of(chunk * CHUNK, CHUNK)
        latents[step, pl.ds(start, CHUNK), :] = fresh
        ours = dot(fresh, p_sender[step]).astype(BF16)
        mesh_visible[step, pl.ds(nodes + start, CHUNK), :] = ours

        @pl.when(chunk == 0)
        def _():
            at = pl.multiple_of(3 * nodes + me * COARSE_ROWS, COARSE_ROWS)
            mesh_visible[step, pl.ds(at, COARSE_ROWS), :] = ours[:COARSE_ROWS]

            def send(by, carry):
                far_copy(step, by, me).start()
                return carry

            lax.fori_loop(1, peers, send, 0)

        for side in range(2):
            near_copy(step, chunk, side).start()

    def encode(chunk, carry):
        rows = pl.ds(pl.multiple_of(chunk * CHUNK, CHUNK), CHUNK)
        fresh = node_chunk(
            rows, CHUNK, degrees[0], visible, meta, 0, degrees[0] + degrees[1], hot, pulled,
            own_term, mesh_lat, e_geometry, e_edge, e_gather, e_output,
        )
        hand_on(0, chunk, fresh)
        return carry

    lax.fori_loop(0, chunks, encode, 0)

    for name in (8, 12, 9, 10, 11, 13):
        loads[name].wait()
    for step in range(steps):
        pulled[...] = dot(latents[step], p_receiver[step])
        own_term[...] = dot(latents[step], p_self[step])

        def settle_near(chunk, carry):
            for side in range(2):
                near_copy(step, chunk, side).wait()
            return carry

        lax.fori_loop(0, chunks, settle_near, 0)

        def settle_far(by, carry):
            far_copy(step, by, me).wait_send()
            far_copy(step, by, peer(-by)).wait_recv()
            return carry

        lax.fori_loop(1, peers, settle_far, 0)

        def process(chunk, carry):
            rows = pl.ds(pl.multiple_of(chunk * CHUNK, CHUNK), CHUNK)
            fresh = node_chunk(
                rows, CHUNK, degrees[1], mesh_visible.at[step], meta, degrees[0],
                5 * degrees[0] + degrees[1], hot, pulled, own_term, latents.at[step],
                p_geometry.at[step], p_edge.at[step], p_gather.at[step], p_output.at[step],
            )
            if step + 1 < steps:
                hand_on(step + 1, chunk, fresh)
            else:
                out_ref[rows, :] = fresh
            return carry

        lax.fori_loop(0, chunks, process, 0)


def local(
    grid_latents, mesh_latents, send_block, send_live, grid_edge_source, grid_edge_geometry,
    mesh_edge_source, mesh_edge_geometry, *weights,
):
    peers = lax.axis_size("lon")
    width = grid_latents.shape[1]
    nodes = mesh_latents.shape[0]
    slots = send_block.shape[1]
    steps = weights[7].shape[0]
    degrees = (grid_edge_source.shape[0] // nodes, mesh_edge_source.shape[0] // nodes)
    far = mesh_edge_source - 3 * nodes
    placed = jnp.where(
        far < 0,
        mesh_edge_source,
        3 * nodes + (far // COARSE_DEV) * COARSE_ROWS + far % COARSE_DEV,
    )
    meta = jnp.concatenate(
        [
            grid_edge_source.reshape(nodes, -1).astype(F32),
            placed.reshape(nodes, -1).astype(F32),
        ]
        + [grid_edge_geometry[k].reshape(nodes, -1) for k in range(4)]
        + [mesh_edge_geometry[k].reshape(nodes, -1) for k in range(4)],
        axis=1,
    )
    meta = jnp.pad(meta, ((0, 0), (0, -meta.shape[1] % 128)))
    table = 3 * nodes + peers * COARSE_ROWS
    grid_rows = grid_latents.shape[0]
    chunks = nodes // CHUNK
    deepest = max(grid_rows + slots * BLOCK, table)
    chosen = (send_block[:, :, None] == jnp.arange(grid_rows // BLOCK)) * send_live[:, :, None]
    held = [meta, grid_latents, mesh_latents, *weights]
    return pl.pallas_call(
        functools.partial(kernel, peers, steps, degrees),
        out_shape=jax.ShapeDtypeStruct(mesh_latents.shape, BF16),
        in_specs=[pl.BlockSpec(memory_space=pltpu.SMEM)]
        + [pl.BlockSpec(memory_space=pl.ANY)] * 17,
        out_specs=pl.BlockSpec(memory_space=pltpu.VMEM),
        scratch_shapes=[pltpu.VMEM(a.shape, a.dtype) for a in held]
        + [
            pltpu.VMEM((grid_rows + slots * BLOCK, width), BF16),
            pltpu.VMEM((slots * BLOCK, width), BF16),
            pltpu.VMEM((steps, table, width), BF16),
            pltpu.VMEM((steps, nodes, width), BF16),
            pltpu.VMEM((nodes, width), F32),
            pltpu.VMEM((nodes, width), F32),
            pltpu.VMEM((CHUNK * max(degrees), deepest), BF16),
            pltpu.SemaphoreType.DMA((17,)),
            pltpu.SemaphoreType.DMA((slots,)),
            pltpu.SemaphoreType.DMA((slots,)),
            pltpu.SemaphoreType.DMA((steps, 2, chunks)),
            pltpu.SemaphoreType.DMA((steps, 2, chunks)),
            pltpu.SemaphoreType.DMA((steps, peers)),
            pltpu.SemaphoreType.DMA((steps, peers)),
        ],
        compiler_params=pltpu.CompilerParams(
            collective_id=0, has_side_effects=True, vmem_limit_bytes=56 * 1024 * 1024
        ),
    )(chosen.astype(F32), *held)


def solution(mesh):
    spread = P(("parts", "lon"), None)
    placed = (
        spread, spread, spread, spread,
        P(("parts", "lon")), P(None, ("parts", "lon")),
        P(("parts", "lon")), P(None, ("parts", "lon")),
    ) + (P(),) * 14
    return jax.shard_map(
        local, mesh=mesh, in_specs=placed, out_specs=spread, check_vma=False
    )
```

time: 156 us -> 72.4 us (0.46)
  Pallas kernels: 0 us -> 63.8 us
  matrix products: 45.8 us -> 0 us
  blocking collectives: 39.4 us -> 0 us
  local copies, waits for them, and re-layouts: 36.3 us -> 7.44 us
  starting transfers between devices: 19.5 us -> 0 us
  other arithmetic: 13.6 us -> 0.66 us
    pallas_call x0 -> x1, Pallas kernels: none -> 63.8 us  [local(): pl.pallas_call(functools.partial(kernel, peers, steps, degrees), out_shap...]
    dot_general x18 -> x0, matrix products: 45.8 us -> none  [the longest x3 20.9 us: interact(): jnp.einsum('ke,kd->ed', geometry, w_geometry, precision=lax.Precision.HIG...]
    all_gather x2 -> x0, blocking collectives: 39.4 us -> none  [local(): lax.all_gather(mesh_projected[:COARSE_DEV], 'lon', axis=0, tiled=True)]
    gather x4 -> x0, local copies, waits for them, and re-layouts: 36.2 us -> none  [the longest x3 35.6 us: interact(): visible[source].astype(jnp.float32) + spread_pull + shape_term]
    ppermute x8 -> x0, starting transfers between devices: 19.5 us -> none  [the longest x4 10.5 us: shifted(): lax.ppermute(array, axis, [(i, (i + by) % peers) for i in range(peers)])]
    reduce_sum x9 -> x0, other arithmetic: 9.3 us -> none  [the longest x3 5.58 us: interact(): jnp.sum(message.astype(jnp.float32).reshape(node_count, degree, width), a...]
    unnamed x34 -> x11, local copies, waits for them, and re-layouts: 0.08 us -> 4.2 us
  transfers between devices with their start and end apart: 8 -> 0, of which waited for: 0 -> 0; matrix products, arithmetic and copies ran while one was open for 8% -> 0% of each run, Pallas kernels for 0% -> 0%
where the time goes in v1:
time: 72.4 us; the launch traced here: 72 us
  Pallas kernels  63.8 us (88%)
  local copies, waits for them, and re-layouts  7.44 us (10%)
    pallas_call x1, Pallas kernels, local(): pl.pallas_call(functools.partial(kernel, peers, steps, degrees), out_shap...  63.8 us
    unnamed x11, local copies, waits for them, and re-layouts  4.2 us

profile of v1, /device:TPU:0, one launch (start us, length us, event | category | flops | bytes accessed | tf_op | source)
XLA Modules:
  0.0 72.0 jit_solution(18396112462711005075)
XLA Ops:
  0.0 1.2 %slice_reduce_fusion = (f32[4096]{0:T(1024)S(1)}, f32[4096]{0:T(1024)S(1)}, f32[4096]{0:T(1024)S(1)}, f32[4096]{0:T(1024)S(1)}) fusion(f32[4,4096]{1,0:T(4,128)} %param.27), kind=kLoop, calls=%fused_computation | loop fusion | bytes 131072 | tf_op jit(solution)/shard_map/slice | solution.py:255
  1.2 0.1 reshape_squeeze.24
  1.3 0.1 reshape_squeeze.25
  1.4 0.1 reshape_squeeze.26
  1.5 0.0 copy-start
  1.5 0.1 reshape_squeeze.27
  1.6 0.7 copy-done
  2.2 0.1 slice_reduce_fusion.4
  2.3 0.1 reshape_squeeze.28
  2.4 0.1 reshape_squeeze.29
  2.5 0.1 reshape_squeeze.30
  2.6 0.0 copy-start.1
  2.6 0.1 reshape_squeeze.31
  2.7 0.6 copy-done.1
  3.4 0.0 copy-start.2
  3.4 0.1 convert_element_type.20
  3.5 0.6 copy-done.2
  4.1 0.1 convert_element_type.22
  4.2 0.4 concatenate.3
  4.6 0.7 pad.4.meta_in
  5.2 0.0 copy-start.3
  5.2 0.0 copy-start.4
  5.2 0.7 copy-done.3
  5.9 0.0 copy-done.4
  5.9 0.6 select_convert_fusion.chosen
  6.6 63.8 %shard_map.214 = bf16[256,512]{1,0:T(8,128)(2,1)} custom-call(f32[1,4,8]{2,1,0:T(4,128)} %select_convert_fusion.chosen, f32[256,128]{1,0:T(8,128)} %pad.4.meta_in, bf16[1024,512]{1,0:T(8,128)(2,1)} %grid_in.1, bf16[256,512]{1,0:T(8,128)(2,1)} %mesh_in.1, bf16[512,512]{1,0:T(8,128)(2,1)} %rest_0_.1, bf16[512,512]{1,0:T(8,128)(2,1)} %rest_1_.1, ...), custom_call_target="tpu_custom_call" | custom-call | tf_op jit(solution)/shard_map/pallas_call | solution.py:266
  70.3 1.7 %copy.24 = bf16[256,512]{1,0:T(8,128)(2,1)} copy(bf16[256,512]{1,0:T(8,128)(2,1)} %shard_map.214) | data formatting | bytes 524288
  (2 shorter events, 0.0 us)
Async XLA Ops:
  1.5 0.8 %copy-start = (f32[4,2048]{1,0:T(4,128)S(1)}, f32[4,2048]{1,0:T(4,128)}, u32[]{:S(2)}) copy-start(f32[4,2048]{1,0:T(4,128)} %param.29) | copy-start | bytes 98308
  2.6 0.7 %copy-start.1 = (s32[4096]{0:T(1024)S(1)}, s32[4096]{0:T(1024)}, u32[]{:S(2)}) copy-start(s32[4096]{0:T(1024)} %param.26) | copy-start | bytes 49156
  3.4 0.7 copy-start.2
  5.2 0.7 copy-start.3
  5.2 0.7 copy-start.4

commit v2 on v1

v2 whole, which is shorter than its diff:
```python
import functools

import jax
import jax.numpy as jnp
from jax import lax
from jax.experimental import pallas as pl
from jax.experimental.pallas import tpu as pltpu
from jax.sharding import PartitionSpec as P

BLOCK = 128
COARSE_DEV = 8
COARSE_ROWS = 16
F32 = jnp.float32
BF16 = jnp.bfloat16


def dot(a, b):
    return jnp.dot(a, b, preferred_element_type=F32)


def silu(v):
    half = 0.5 * v
    return half + half * jnp.tanh(half)


def layer_norm(v):
    centred = v - jnp.mean(v, axis=-1, keepdims=True)
    spread = jnp.mean(centred * centred, axis=-1, keepdims=True)
    return centred * lax.rsqrt(spread + 1e-05)


PARTS = 3


def one_hot(index_ref, rows, n, degree, first, depth, hot):
    index = index_ref[rows, :]
    lane = lax.broadcasted_iota(jnp.int32, (n, 128), 1) + first
    for j in range(degree):
        away = (jnp.broadcast_to(index[:, j : j + 1], (n, 128)) - lane).astype(jnp.int16)
        for tile in range(depth // 128):
            hot[j * n : (j + 1) * n, tile * 128 : (tile + 1) * 128] = jnp.where(
                away == jnp.int16(tile * 128), jnp.array(1, BF16), jnp.array(0, BF16)
            )


def geometry_rows(w_geometry, degree, depth):
    w = w_geometry[...]
    high = w.astype(BF16).astype(F32)
    rows = [
        jnp.broadcast_to(part[k : k + 1], (degree, w.shape[1]))
        for part in (high, high, w - high)
        for k in range(4)
    ]
    rows.append(jnp.zeros((depth - PARTS * 4 * degree, w.shape[1]), F32))
    return jnp.concatenate(rows, axis=0).astype(BF16)


def geometry_columns(geometry_ref, rows, n, degree, at, hot):
    value = geometry_ref[rows, :]
    depth = value.shape[1]
    lane = lax.broadcasted_iota(jnp.int32, value.shape, 1)
    high = value.astype(BF16).astype(F32)
    part = jnp.where((lane >= 4 * degree) & (lane < 8 * degree), value - high, high)
    turn = lane % degree
    for j in range(degree):
        hot[j * n : (j + 1) * n, at : at + depth] = jnp.where(turn == j, part, 0.0).astype(BF16)


def pick_early(rows, n, degree, table, first_geometry, index_ref, geometry_ref, hot, picked, chunk):
    depth = geometry_ref.shape[1]
    one_hot(index_ref, rows, n, degree, 0, first_geometry, hot)
    geometry_columns(geometry_ref, rows, n, degree, first_geometry, hot)
    width = first_geometry + depth
    picked[pl.ds(pl.multiple_of(chunk * n * degree, 128), n * degree), :] = dot(
        hot[: n * degree, :width], table[:width, :]
    )


def node_chunk(
    rows, n, degree, table, late, index_ref, hot, picked, chunk, pulled, own_term, receivers,
    w_edge, w_gather, w_output,
):
    depth = table.shape[0] - late
    one_hot(index_ref, rows, n, degree, late, depth, hot)
    term = picked[pl.ds(pl.multiple_of(chunk * n * degree, 128), n * degree), :]
    term = term + dot(hot[: degree * n, :depth], table[late:, :])
    base = pulled[rows, :]
    joined = [silu(term[j * n : (j + 1) * n] + base).astype(BF16) for j in range(degree)]
    message = layer_norm(dot(jnp.concatenate(joined, axis=0), w_edge[...]))
    summed = message[:n]
    for j in range(1, degree):
        summed = summed + message[j * n : (j + 1) * n]
    update = silu(dot(summed.astype(BF16), w_gather[...]) + own_term[rows, :]).astype(BF16)
    out = layer_norm(dot(update, w_output[...]))
    return (receivers[rows, :].astype(F32) + out).astype(BF16)


def kernel(
    peers, steps, degrees,
    chosen, index_g_in, index_m_in, geometry_g_in, geometry_m_in, grid_in, mesh_in, *rest,
):
    weights_in = rest[:14]
    out_ref = rest[14]
    (index_g, index_m, geometry_g, geometry_m, grid, mesh_lat, *weights) = rest[15 : 15 + 20]
    (
        visible, outgoing, mesh_visible, latents, pulled, own_term, hot, picked,
        load_sem, slot_send, slot_recv, near_send, near_recv, far_send, far_recv,
    ) = rest[35:]
    (
        e_sender, e_receiver, e_geometry, e_edge, e_gather, e_self, e_output,
        p_sender, p_receiver, p_geometry, p_edge, p_gather, p_self, p_output,
    ) = weights
    me = lax.axis_index("lon")
    slots = outgoing.shape[0] // BLOCK
    offsets = [(s // 2 + 1) * (1 - 2 * (s % 2)) for s in range(slots)]
    nodes = mesh_lat.shape[0]
    grid_rows = grid.shape[0]
    chunks = 2
    half = nodes // chunks
    degree_g, degree_m = degrees
    slot_base = grid_rows + geometry_g.shape[1]
    far_base = 2 * nodes
    geometry_base = far_base + peers * COARSE_ROWS
    late_base = geometry_base + geometry_m.shape[1]

    def peer(by):
        return lax.rem(me + by + peers, peers)

    barrier = pltpu.get_barrier_semaphore()

    def greet(by, carry):
        pl.semaphore_signal(
            barrier, inc=1, device_id={"lon": peer(by)}, device_id_type=pl.DeviceIdType.MESH
        )
        return carry

    lax.fori_loop(1, peers, greet, 0)

    loads = {}
    pairs = {"grid": (grid_in, grid), "mesh": (mesh_in, mesh_lat)}
    pairs["ig"] = (index_g_in, index_g)
    pairs["im"] = (index_m_in, index_m)
    pairs["gg"] = (geometry_g_in, geometry_g)
    pairs["gm"] = (geometry_m_in, geometry_m)
    for at in range(14):
        pairs[at] = (weights_in[at], weights[at])
    order = ["grid", 0, "mesh", 1, 5, 2, "ig", "gg", 3, 4, 6, 7, 9, 8, 12, "im", "gm", 10, 11, 13]
    for at, name in enumerate(order):
        loads[name] = pltpu.make_async_copy(*pairs[name], load_sem.at[at])
        loads[name].start()

    loads["grid"].wait()
    loads[0].wait()
    w_sender = e_sender[...]
    for s in range(slots):
        total = None
        for b in range(grid_rows // BLOCK):
            part = grid[b * BLOCK : (b + 1) * BLOCK, :].astype(F32) * chosen[0, s, b]
            total = part if total is None else total + part
        outgoing[s * BLOCK : (s + 1) * BLOCK, :] = dot(total.astype(BF16), w_sender).astype(BF16)
    pl.semaphore_wait(barrier, peers - 1)
    slot_copies = []
    for s in range(slots):
        copy = pltpu.make_async_remote_copy(
            src_ref=outgoing.at[pl.ds(s * BLOCK, BLOCK)],
            dst_ref=visible.at[pl.ds(slot_base + s * BLOCK, BLOCK)],
            send_sem=slot_send.at[s],
            recv_sem=slot_recv.at[s],
            device_id={"lon": peer(offsets[s])},
            device_id_type=pl.DeviceIdType.MESH,
        )
        copy.start()
        slot_copies.append(copy)
    visible[:grid_rows, :] = dot(grid[...], w_sender).astype(BF16)
    loads["mesh"].wait()
    loads[1].wait()
    pulled[...] = dot(mesh_lat[...], e_receiver[...])
    loads[5].wait()
    own_term[...] = dot(mesh_lat[...], e_self[...])
    for name in (2, "ig", "gg"):
        loads[name].wait()
    visible[grid_rows:slot_base, :] = geometry_rows(e_geometry, degree_g, slot_base - grid_rows)

    def rows_of(chunk):
        return pl.ds(pl.multiple_of(chunk * half, half), half)

    def early_g(chunk, carry):
        pick_early(
            rows_of(chunk), half, degree_g, visible, grid_rows, index_g, geometry_g, hot, picked, chunk
        )
        return carry

    lax.fori_loop(0, chunks, early_g, 0)
    for name in (3, 4, 6, 7, 9):
        loads[name].wait()
    for copy in slot_copies:
        copy.wait()

    def near_copy(step, chunk, side):
        landing = (nodes if chunk == 0 else late_base) + side * half
        return pltpu.make_async_remote_copy(
            src_ref=mesh_visible.at[step, pl.ds(chunk * half, half)],
            dst_ref=mesh_visible.at[step, pl.ds(landing, half)],
            send_sem=near_send.at[step, side, chunk],
            recv_sem=near_recv.at[step, side, chunk],
            device_id={"lon": peer(1 if side == 0 else -1)},
            device_id_type=pl.DeviceIdType.MESH,
        )

    def far_copy(step, by, sender):
        start = pl.multiple_of(far_base + sender * COARSE_ROWS, COARSE_ROWS)
        return pltpu.make_async_remote_copy(
            src_ref=mesh_visible.at[step, pl.ds(0, COARSE_ROWS)],
            dst_ref=mesh_visible.at[step, pl.ds(start, COARSE_ROWS)],
            send_sem=far_send.at[step, by],
            recv_sem=far_recv.at[step, sender],
            device_id={"lon": peer(by)},
            device_id_type=pl.DeviceIdType.MESH,
        )

    def hand_on(step, chunk, fresh):
        rows = rows_of(chunk)
        latents[step, rows, :] = fresh
        ours = dot(fresh, p_sender[step]).astype(BF16)
        mesh_visible[step, rows, :] = ours

        @pl.when(chunk == 0)
        def _():
            for side in range(2):
                near_copy(step, 0, side).start()
            at = pl.multiple_of(far_base + me * COARSE_ROWS, COARSE_ROWS)
            mesh_visible[step, pl.ds(at, COARSE_ROWS), :] = ours[:COARSE_ROWS]

            def send(by, carry):
                far_copy(step, by, me).start()
                return carry

            lax.fori_loop(1, peers, send, 0)

        @pl.when(chunk == 1)
        def _():
            for side in range(2):
                near_copy(step, 1, side).start()

    def encode(chunk, carry):
        fresh = node_chunk(
            rows_of(chunk), half, degree_g, visible, slot_base, index_g, hot, picked, chunk, pulled,
            own_term, mesh_lat, e_edge, e_gather, e_output,
        )
        hand_on(0, chunk, fresh)
        return carry

    lax.fori_loop(0, chunks, encode, 0)

    for name in (8, 12, "im", "gm", 10, 11, 13):
        loads[name].wait()
    for step in range(steps):
        table = mesh_visible.at[step]
        pulled[...] = dot(latents[step], p_receiver[step])
        own_term[...] = dot(latents[step], p_self[step])
        table[geometry_base:late_base, :] = geometry_rows(
            p_geometry.at[step], degree_m, late_base - geometry_base
        )
        for side in range(2):
            near_copy(step, 0, side).wait()

        def settle_far(by, carry):
            far_copy(step, by, me).wait_send()
            far_copy(step, by, peer(-by)).wait_recv()
            return carry

        lax.fori_loop(1, peers, settle_far, 0)

        def early_m(chunk, carry):
            pick_early(
                rows_of(chunk), half, degree_m, table, geometry_base, index_m, geometry_m, hot,
                picked, chunk,
            )
            return carry

        lax.fori_loop(0, chunks, early_m, 0)
        for side in range(2):
            near_copy(step, 1, side).wait()

        def process(chunk, carry):
            fresh = node_chunk(
                rows_of(chunk), half, degree_m, table, late_base, index_m, hot, picked, chunk,
                pulled, own_term, latents.at[step], p_edge.at[step], p_gather.at[step],
                p_output.at[step],
            )
            if step + 1 < steps:
                hand_on(step + 1, chunk, fresh)
            else:
                out_ref[rows_of(chunk), :] = fresh
            return carry

        lax.fori_loop(0, chunks, process, 0)


def spread_geometry(geometry, nodes, degree):
    flat = geometry.reshape(4, nodes, degree).transpose(1, 0, 2).reshape(nodes, 4 * degree)
    blank = jnp.zeros((nodes, -PARTS * 4 * degree % 128), F32)
    return jnp.concatenate([flat] * PARTS + [blank], axis=1)


def local(
    grid_latents, mesh_latents, send_block, send_live, grid_edge_source, grid_edge_geometry,
    mesh_edge_source, mesh_edge_geometry, *weights,
):
    peers = lax.axis_size("lon")
    width = grid_latents.shape[1]
    nodes = mesh_latents.shape[0]
    slots = send_block.shape[1]
    steps = weights[7].shape[0]
    degrees = (grid_edge_source.shape[0] // nodes, mesh_edge_source.shape[0] // nodes)
    grid_rows = grid_latents.shape[0]
    geometry_g = spread_geometry(grid_edge_geometry, nodes, degrees[0])
    geometry_m = spread_geometry(mesh_edge_geometry, nodes, degrees[1])
    index_g = jnp.where(
        grid_edge_source < grid_rows, grid_edge_source, grid_edge_source + geometry_g.shape[1]
    ).reshape(nodes, -1)
    half = nodes // 2
    far_base = 2 * nodes
    late_base = far_base + peers * COARSE_ROWS + geometry_m.shape[1]
    part, within = mesh_edge_source // nodes, mesh_edge_source % nodes
    beside = jnp.where(within < half, nodes + within, late_base + within - half)
    beside = jnp.where(part == 2, beside + half, beside)
    far = mesh_edge_source - 3 * nodes
    index_m = jnp.where(
        part == 1,
        within,
        jnp.where(
            part < 3, beside, far_base + (far // COARSE_DEV) * COARSE_ROWS + far % COARSE_DEV
        ),
    ).reshape(nodes, -1)
    table_g = grid_rows + geometry_g.shape[1] + slots * BLOCK
    table_m = late_base + nodes
    chunks = 2
    chosen = (send_block[:, :, None] == jnp.arange(grid_rows // BLOCK)) * send_live[:, :, None]
    held = [index_g, index_m, geometry_g, geometry_m, grid_latents, mesh_latents, *weights]
    return pl.pallas_call(
        functools.partial(kernel, peers, steps, degrees),
        out_shape=jax.ShapeDtypeStruct(mesh_latents.shape, BF16),
        in_specs=[pl.BlockSpec(memory_space=pltpu.SMEM)]
        + [pl.BlockSpec(memory_space=pl.ANY)] * 20,
        out_specs=pl.BlockSpec(memory_space=pltpu.VMEM),
        scratch_shapes=[pltpu.VMEM(a.shape, a.dtype) for a in held]
        + [
            pltpu.VMEM((table_g, width), BF16),
            pltpu.VMEM((slots * BLOCK, width), BF16),
            pltpu.VMEM((steps, table_m, width), BF16),
            pltpu.VMEM((steps, nodes, width), BF16),
            pltpu.VMEM((nodes, width), F32),
            pltpu.VMEM((nodes, width), F32),
            pltpu.VMEM((half * max(degrees), max(table_g, table_m)), BF16),
            pltpu.VMEM((nodes * max(degrees), width), F32),
            pltpu.SemaphoreType.DMA((20,)),
            pltpu.SemaphoreType.DMA((slots,)),
            pltpu.SemaphoreType.DMA((slots,)),
            pltpu.SemaphoreType.DMA((steps, 2, chunks)),
            pltpu.SemaphoreType.DMA((steps, 2, chunks)),
            pltpu.SemaphoreType.DMA((steps, peers)),
            pltpu.SemaphoreType.DMA((steps, peers)),
        ],
        compiler_params=pltpu.CompilerParams(
            collective_id=0, has_side_effects=True, vmem_limit_bytes=56 * 1024 * 1024
        ),
    )(chosen.astype(F32), *held)


def solution(mesh):
    spread = P(("parts", "lon"), None)
    placed = (
        spread, spread, spread, spread,
        P(("parts", "lon")), P(None, ("parts", "lon")),
        P(("parts", "lon")), P(None, ("parts", "lon")),
    ) + (P(),) * 14
    return jax.shard_map(
        local, mesh=mesh, in_specs=placed, out_specs=spread, check_vma=False
    )
```

time: 72.4 us -> 60.6 us (0.84)
  Pallas kernels: 63.8 us -> 51.6 us
  other arithmetic: 0.66 us -> 2.31 us
  local copies, waits for them, and re-layouts: 7.44 us -> 5.9 us
    pallas_call x1, Pallas kernels: 63.8 us -> 51.6 us  [local(): pl.pallas_call(functools.partial(kernel, peers, steps, degrees), out_shap...]
    reshape x0 -> x6, local copies, waits for them, and re-layouts: none -> 3.07 us  [the longest x4 1.55 us: spread_geometry(): geometry.reshape(4, nodes, degree).transpose(1, 0, 2)]
    unnamed x11, local copies, waits for them, and re-layouts: 4.2 us -> 2.35 us
    concatenate x0 -> x2, other arithmetic: none -> 1.63 us  [spread_geometry(): return jnp.concatenate([flat] * PARTS + [blank], axis=1)]
    slice x2 -> x0, local copies, waits for them, and re-layouts: 1.25 us -> none  [the longest x1 1.17 us: local(): grid_edge_geometry[k].reshape(nodes, -1)]
    another operation x8 -> x0, local copies, waits for them, and re-layouts: 0.75 us -> none  [the longest x4 0.39 us: local(): mesh_edge_geometry[k].reshape(nodes, -1)]
where the time goes in v2:
time: 60.6 us; the launch traced here: 59.9 us
  Pallas kernels  51.6 us (85%)
  local copies, waits for them, and re-layouts  5.9 us (10%)
  other arithmetic  2.31 us (4%)
    pallas_call x1, Pallas kernels, local(): pl.pallas_call(functools.partial(kernel, peers, steps, degrees), out_shap...  51.6 us
    unnamed x11, local copies, waits for them, and re-layouts  2.35 us
    concatenate x2, other arithmetic, spread_geometry(): return jnp.concatenate([flat] * PARTS + [blank], axis=1)  1.63 us
    reshape x4, local copies, waits for them, and re-layouts, spread_geometry(): geometry.reshape(4, nodes, degree).transpose(1, 0, 2)  1.55 us

profile of v2, /device:TPU:0, one launch (start us, length us, event | category | flops | bytes accessed | tf_op | source)
XLA Modules:
  0.0 59.9 jit_solution(8841363347443068567)
XLA Ops:
  0.0 1.0 %reshape.94 = f32[4,256,16]{2,1,0:T(8,128)S(1)} reshape(f32[4,4096]{1,0:T(4,128)} %param.27) | data formatting | bytes 131072 | tf_op jit(solution)/shard_map/reshape | solution.py:301
  1.1 0.2 copy.25
  1.2 0.1 copy.26
  1.3 0.1 pad.7.clone
  1.4 0.0 copy-start
  1.4 0.8 %maximum_maximum_fusion.geometry_g_in = f32[256,256]{1,0:T(8,128)} fusion(f32[256,64]{1,0:T(8,128)S(1)} %copy.26, f32[256]{0:T(256)S(1)} %pad.7.clone), kind=kLoop, calls=%fused_computation | loop fusion | flops 196608 | bytes 328704 | tf_op jit(solution)/shard_map/concatenate | solution.py:303
  2.3 0.0 copy-done
  2.3 0.3 reshape.96
  2.6 0.2 copy.29
  2.7 0.1 copy.30
  2.9 0.1 pad.3.clone
  2.9 0.0 copy-start.1
  2.9 0.8 %maximum_maximum_fusion.1.geometry_m_in = f32[256,128]{1,0:T(8,128)} fusion(f32[256,32]{1,0:T(8,128)S(1)} %copy.30, f32[128]{0:T(128)S(1)} %pad.3.clone), kind=kLoop, calls=%fused_computation.1 | loop fusion | flops 98304 | bytes 164352 | tf_op jit(solution)/shard_map/concatenate | solution.py:303
  3.7 0.0 copy-done.1
  3.7 0.0 copy-start.2
  3.7 0.7 %reshape.92.index_g_in = s32[256,16]{1,0:T(8,128)} reshape(s32[4096]{0:T(1024)S(1)} %compare_select_fusion) | data formatting | bytes 32768 | tf_op jit(solution)/shard_map/reshape | solution.py:321
  4.5 0.0 copy-done.2
  4.5 0.8 %reshape.93.index_m_in = s32[256,8]{1,0:T(8,128)} reshape(s32[2048]{0:T(1024)S(1)} %fusion.1) | data formatting | bytes 16384 | tf_op jit(solution)/shard_map/reshape | solution.py:335
  5.3 0.0 copy-start.3
  5.3 0.0 copy-start.4
  5.3 0.7 %copy-done.3 = s32[1,4]{1,0:T(1,128)S(1)} copy-done((s32[1,4]{1,0:T(1,128)S(1)}, s32[1,4]{1,0:T(1,128)}, u32[]{:S(2)}) %copy-start.3) | copy-done | bytes 40
  5.9 0.0 copy-done.4
  5.9 0.7 %select_convert_fusion.chosen = f32[1,4,8]{2,1,0:T(4,128)} fusion(s32[4]{0:T(128)S(1)} %bitcast.10, s32[4]{0:T(128)S(1)} %bitcast.11), kind=kLoop, calls=%fused_computation.26 | loop fusion | flops 96 | bytes 160 | tf_op jit(solution)/shard_map/convert_element_type | solution.py:368
  6.6 51.6 %shard_map.214 = bf16[256,512]{1,0:T(8,128)(2,1)} custom-call(f32[1,4,8]{2,1,0:T(4,128)} %select_convert_fusion.chosen, s32[256,16]{1,0:T(8,128)} %reshape.92.index_g_in, s32[256,8]{1,0:T(8,128)} %reshape.93.index_m_in, f32[256,256]{1,0:T(8,128)} %maximum_maximum_fusion.geometry_g_in, f32[256,128]{1,0:T(8,128)} %maximum_maximum_fusion.1.geometry_m_in, ...), custom_call_target="tpu_custom_call" | custom-call | tf_op jit(solution)/shard_map/pallas_call | solution.py:341
  58.2 1.7 %copy.34 = bf16[256,512]{1,0:T(8,128)(2,1)} copy(bf16[256,512]{1,0:T(8,128)(2,1)} %shard_map.214) | data formatting | bytes 524288
  (4 shorter events, 0.0 us)
Async XLA Ops:
  1.4 0.8 %copy-start = (f32[4,2048]{1,0:T(4,128)S(1)}, f32[4,2048]{1,0:T(4,128)}, u32[]{:S(2)}) copy-start(f32[4,2048]{1,0:T(4,128)} %param.29) | copy-start | bytes 98308
  2.9 0.8 %copy-start.1 = (s32[4096]{0:T(1024)S(1)}, s32[4096]{0:T(1024)}, u32[]{:S(2)}) copy-start(s32[4096]{0:T(1024)} %param.26) | copy-start | bytes 49156
  3.7 0.8 %copy-start.2 = (s32[2048]{0:T(1024)S(1)}, s32[2048]{0:T(1024)}, u32[]{:S(2)}) copy-start(s32[2048]{0:T(1024)} %param.28) | copy-start | bytes 24580
  5.3 0.7 %copy-start.3 = (s32[1,4]{1,0:T(1,128)S(1)}, s32[1,4]{1,0:T(1,128)}, u32[]{:S(2)}) copy-start(s32[1,4]{1,0:T(1,128)} %param.25) | copy-start | bytes 52
  5.3 0.7 %copy-start.4 = (s32[1,4]{1,0:T(1,128)S(1)}, s32[1,4]{1,0:T(1,128)}, u32[]{:S(2)}) copy-start(s32[1,4]{1,0:T(1,128)} %param.24) | copy-start | bytes 52
